TPU v7x, 256 devices: a whole 4x4x8 slice. The times are simulated.
256 devices in a mesh: img: 32 (over z, x), txt: 8 (over y, core).
Axes of the slice: x: 4, y: 4, z: 8, core: 2. Of those that a mesh axis runs over, the one named last changes fastest.
Arguments:
- image_pooled: bfloat16 [16384, 1664], P('img', 'txt'), may hold values from -6 to 6
- text_pooled: bfloat16 [16384, 1280], P('txt', 'img'), may hold values from -6 to 6
- image_proj: bfloat16 [1664, 1280], P('txt'), may hold values from -1.5 to 1.5
- text_proj: bfloat16 [1280, 1280], P('img'), may hold values from -2 to 2
- teacher_scale: float32 [1], replicated, may hold values from 280 to 400
Outputs:
- image_targets: float32 [16384, 16384], P('img', 'txt')
- text_targets: float32 [16384, 16384], P('img', 'txt')
All inputs are finite; a program needn't handle non-finite values.
Results may differ from a plain program's by a relative error of at most 0.0011.
Values may be sent and summed in bfloat16 or wider, within the bound.
No kernel may reach another device: no remote copies, remote signals or barrier semaphores. Data moves between devices by JAX's collectives and lax.ppermute only.
A program may use at most 64 MiB of HBM per device.

v0:
```python
import math
import jax
import jax.numpy as jnp
from jax import lax
from jax.sharding import PartitionSpec as P


def unit_rows(values):
    scale_rows = lax.rsqrt(jnp.mean(values * values, axis=-1, keepdims=True) + 1e-06)
    return (values * scale_rows / math.sqrt(values.shape[-1])).astype(jnp.bfloat16)


def add_rows(left_side, portion):
    return jnp.dot(left_side, portion, preferred_element_type=jnp.float32)


def on_device(image_pooled, text_pooled, image_proj, text_proj, teacher_scale):
    image_full = lax.all_gather(image_pooled, "txt", axis=1, tiled=True)
    image_sum = add_rows(image_full, lax.all_gather(image_proj, "txt", axis=0, tiled=True))
    image_unit = unit_rows(image_sum)
    weight_full = lax.all_gather(text_proj, "img", axis=0, tiled=True)
    text_full = lax.all_gather(text_pooled, "img", axis=1, tiled=True)
    text_unit = unit_rows(jnp.dot(text_full, weight_full, preferred_element_type=jnp.float32))
    similar = lax.dot_general(
        image_unit, text_unit, (((1,), (1,)), ((), ())), preferred_element_type=jnp.float32
    )
    logits = teacher_scale[0] * similar
    row_top = jnp.max(logits, axis=1, keepdims=True)
    col_top = jnp.max(logits, axis=0, keepdims=True)
    row_top = lax.pmax(row_top, "txt")
    col_top = lax.pmax(col_top, "img")
    row_total = lax.psum(jnp.sum(jnp.exp(logits - row_top), axis=1, keepdims=True), "txt")
    col_total = lax.psum(jnp.sum(jnp.exp(logits - col_top), axis=0, keepdims=True), "img")
    image_targets = logits - (row_top + jnp.log(row_total))
    text_targets = logits - (col_top + jnp.log(col_total))
    return (image_targets, text_targets)


def solution(mesh):
    placed = (P("img", "txt"), P("txt", "img"), P("txt", None), P("img", None), P())
    return jax.shard_map(
        on_device,
        mesh=mesh,
        in_specs=placed,
        out_specs=(P("img", "txt"), P("img", "txt")),
        check_vma=False,
    )
```

profile of v0, /device:TPU:2, one launch (start us, length us, event | category | flops | bytes accessed | tf_op | source)
XLA Modules:
  0.0 444.3 jit_solution(12399462446347487872)
XLA Ops:
  7.2 0.0 all-gather.5.cloned.1.call-start
  7.2 0.7 all-gather.5.cloned.1.call-update
  7.9 0.0 all-gather.7.cloned.1.call-start
  7.9 0.7 all-gather.7.cloned.1.call-update
  8.6 0.0 all-gather.11.cloned.1.call-start
  8.7 0.7 all-gather.11.cloned.1.call-update
  9.4 0.0 all-gather.9.cloned.1.call-start
  9.4 0.5 all-gather.9.cloned.1.call-update
  10.6 29.3 %all-gather.5.cloned.1.call-done = bf16[512,1664]{0,1:T(8,128)(2,1)} async-done(((bf16[512,208]{0,1:T(8,128)(2,1)}), bf16[512,1664]{0,1:T(8,128)(2,1)}) %all-gather.5.cloned.1.call-update) | async-done | bytes 1703952 | tf_op jit(solution)/shard_map/all_gather | solution.py:18
  39.9 37.1 %all-gather.7.cloned.1.call-done = bf16[1664,1280]{1,0:T(8,128)(2,1)} async-done(((bf16[208,1280]{1,0:T(8,128)(2,1)}), bf16[1664,1280]{1,0:T(8,128)(2,1)}) %all-gather.7.cloned.1.call-update) | async-done | bytes 4259856 | tf_op jit(solution)/shard_map/all_gather | solution.py:19
  77.0 5.5 %multiply_reduce_fusion.1 = (f32[512]{0:T(512)S(1)}, f32[512,1280]{1,0:T(8,128)S(1)}) fusion(bf16[512,1664]{0,1:T(8,128)(2,1)} %all-gather.5.cloned.1.call-done, bf16[1664,1280]{1,0:T(8,128)(2,1)} %all-gather.7.cloned.1.call-done), kind=kOutput, calls=%fused_computation.9 | convolution fusion | flops 2182348288 | bytes 8587264 | tf_op jit(solution)/shard_map/dot_general | solution.py:14
  82.5 76.1 %all-gather.11.cloned.1.call-done = bf16[1280,1280]{1,0:T(8,128)(2,1)} async-done(((bf16[40,1280]{1,0:T(8,128)(2,1)}), bf16[1280,1280]{1,0:T(8,128)(2,1)}) %all-gather.11.cloned.1.call-update) | async-done | bytes 3276816 | tf_op jit(solution)/shard_map/all_gather | solution.py:21
  158.6 84.0 %all-gather.9.cloned.1.call-done = bf16[2048,1280]{0,1:T(8,128)(2,1)} async-done(((bf16[2048,40]{0,1:T(8,128)(2,1)}), bf16[2048,1280]{0,1:T(8,128)(2,1)}) %all-gather.9.cloned.1.call-update) | async-done | bytes 5242896 | tf_op jit(solution)/shard_map/all_gather | solution.py:22
  242.7 10.4 %multiply_reduce_fusion = (f32[2048]{0:T(1024)S(1)}, f32[2048,1280]{0,1:T(8,128)S(1)}) fusion(bf16[2048,1280]{0,1:T(8,128)(2,1)} %all-gather.9.cloned.1.call-done, bf16[1280,1280]{1,0:T(8,128)(2,1)} %all-gather.11.cloned.1.call-done), kind=kOutput, calls=%fused_computation.1 | convolution fusion | flops 6716127232 | bytes 19013632 | tf_op jit(solution)/shard_map/dot_general | solution.py:23
  253.1 4.7 %fusion.7 = (f32[2048]{0:T(1024)S(1)}, f32[512]{0:T(512)S(1)}, f32[512,2048]{1,0:T(8,128)}) fusion(f32[2048,1280]{0,1:T(8,128)S(1)} %get-tuple-element.9, f32[2048]{0:T(1024)S(1)} %add_rsqrt_fusion, f32[512,1280]{1,0:T(8,128)S(1)} %get-tuple-element.11, f32[512]{0:T(512)S(1)} %add_rsqrt_fusion.1, f32[]{:T(128)} %bitcast.13), kind=kOutput, calls=%fused_computation.19 | convolution fusion | flops 2697328128 | bytes 17321988 | tf_op jit(solution)/shard_map/dot_general | solution.py:24
  257.8 72.6 %pmax.15 = f32[1,2048]{1,0:T(1,128)S(1)} all-reduce(f32[1,2048]{1,0:T(1,128)S(1)} %bitcast.20), channel_id=1, replica_groups=mesh['img'=32,'txt'=8] {'img'}, use_global_device_ids=true, to_apply=%region_7.0 | all-reduce | flops 2048 | bytes 16384 | tf_op jit(solution)/shard_map/pmax | solution.py:31
  330.4 12.4 %pmax.14 = f32[512,1]{0,1:T(1,128)S(1)} all-reduce(f32[512,1]{0,1:T(1,128)S(1)} %bitcast.21), channel_id=1, replica_groups=mesh['img'=32,'txt'=8] {'txt'}, use_global_device_ids=true, to_apply=%region_3.0 | all-reduce | flops 512 | bytes 4096 | tf_op jit(solution)/shard_map/pmax | solution.py:30
  342.8 3.4 exponential_reduce_fusion
  346.2 12.4 %psum.14 = f32[512,1]{0,1:T(1,128)S(1)} all-reduce(f32[512,1]{0,1:T(1,128)S(1)} %bitcast.18), channel_id=1, replica_groups=mesh['img'=32,'txt'=8] {'txt'}, use_global_device_ids=true, to_apply=%region_5.0 | all-reduce | flops 512 | bytes 4096 | tf_op jit(solution)/shard_map/psum | solution.py:32
  358.7 73.0 %psum.15 = f32[1,2048]{1,0:T(1,128)S(1)} all-reduce(f32[1,2048]{1,0:T(1,128)S(1)} %bitcast.16), channel_id=1, replica_groups=mesh['img'=32,'txt'=8] {'img'}, use_global_device_ids=true, to_apply=%region_9.0 | all-reduce | flops 2048 | bytes 16384 | tf_op jit(solution)/shard_map/psum | solution.py:33
  431.7 6.1 %broadcast_subtract_fusion = (f32[512,2048]{1,0:T(8,128)}, f32[512,2048]{1,0:T(8,128)}) fusion(f32[512,2048]{1,0:T(8,128)} %get-tuple-element.12, f32[2048]{0:T(1024)S(1)} %bitcast.15, f32[512]{0:T(512)S(1)} %bitcast.19), kind=kLoop, calls=%fused_computation.10 | loop fusion | flops 2097152 | bytes 12593152 | tf_op jit(solution)/shard_map/sub | solution.py:35
  (4 shorter events, 0.0 us)
Async XLA Ops:
  7.2 32.8 %all-gather.5.cloned.1.call-start = ((), (), s32[]{:S(2)}) async-start(), calls=%async_computation | async-start | bytes 1916928 | tf_op jit(solution)/shard_map/all_gather | solution.py:18
  7.9 69.1 %all-gather.7.cloned.1.call-start = ((), (), s32[]{:S(2)}) async-start(), calls=%async_computation.1 | async-start | bytes 4792320 | tf_op jit(solution)/shard_map/all_gather | solution.py:19
  8.6 150.0 %all-gather.11.cloned.1.call-start = ((), (), s32[]{:S(2)}) async-start(), calls=%async_computation.3 | async-start | bytes 3379200 | tf_op jit(solution)/shard_map/all_gather | solution.py:21
  9.4 233.3 %all-gather.9.cloned.1.call-start = ((), (), s32[]{:S(2)}) async-start(), calls=%async_computation.2 | async-start | bytes 5406720 | tf_op jit(solution)/shard_map/all_gather | solution.py:22
Sparse Core Ops, SparseCore 0:
  9.8 30.0 all-gather.4
  41.7 35.2 all-gather.6
  79.6 78.9 all-gather.10
  161.0 81.5 all-gather.8
where the time goes:
time: 445 us; the launch traced here: 444 us
  waiting for transfers between devices  229 us (51%)
  blocking collectives  170 us (38%)
  matrix products  20.6 us (5%)
  between operations  14.4 us (3%)
  other arithmetic  9.6 us (2%)
    all_gather x1, waiting for transfers between devices, on_device(): text_full = lax.all_gather(text_pooled, 'img', axis=1, tiled=True)  84 us
    all_gather x1, waiting for transfers between devices, on_device(): weight_full = lax.all_gather(text_proj, 'img', axis=0, tiled=True)  76.1 us
    psum x1, blocking collectives, on_device(): lax.psum(jnp.sum(jnp.exp(logits - col_top), axis=0, keepdims=True), 'img')  73 us
    pmax x1, blocking collectives, on_device(): col_top = lax.pmax(col_top, 'img')  72.6 us
    all_gather x1, waiting for transfers between devices, on_device(): lax.all_gather(image_proj, 'txt', axis=0, tiled=True)  37.1 us
    all_gather x1, waiting for transfers between devices, on_device(): image_full = lax.all_gather(image_pooled, 'txt', axis=1, tiled=True)  29.3 us
    pmax x1, blocking collectives, on_device(): row_top = lax.pmax(row_top, 'txt')  12.4 us
    psum x1, blocking collectives, on_device(): lax.psum(jnp.sum(jnp.exp(logits - row_top), axis=1, keepdims=True), 'txt')  12.4 us
  transfers between devices with their start and end apart: 4, of which 4 were waited for; matrix products, arithmetic and copies ran while one was open for 1% of the time, Pallas kernels for 0%

commit v1 on v0

--- a/solution.py
+++ b/solution.py
@@ -15,7 +15,10 @@
 
 
 def on_device(image_pooled, text_pooled, image_proj, text_proj, teacher_scale):
-    image_full = lax.all_gather(image_pooled, "txt", axis=1, tiled=True)
+    n_dev = lax.axis_size("txt")
+    parts = jnp.stack([image_pooled for _ in range(n_dev)])
+    parts = lax.all_to_all(parts, "txt", split_axis=0, concat_axis=0)
+    image_full = jnp.concatenate(parts, axis=1)
     image_sum = add_rows(image_full, lax.all_gather(image_proj, "txt", axis=0, tiled=True))
     image_unit = unit_rows(image_sum)
     weight_full = lax.all_gather(text_proj, "img", axis=0, tiled=True)

time: 445 us -> 427 us (0.960)
  waiting for transfers between devices: 229 us -> 204 us
    all_to_all x0 -> x1, waiting for transfers between devices: none -> 32.5 us  [on_device(): parts = lax.all_to_all(parts, 'txt', split_axis=0, concat_axis=0)]
    all_gather x1 -> x0, waiting for transfers between devices: 29.3 us -> none  [on_device(): image_full = lax.all_gather(image_pooled, 'txt', axis=1, tiled=True)]
    all_gather x1, waiting for transfers between devices: 37.1 us -> 8.31 us  [on_device(): lax.all_gather(image_proj, 'txt', axis=0, tiled=True)]
    all_to_all x0 -> x1, starting transfers between devices: none -> 4.47 us  [on_device(): parts = lax.all_to_all(parts, 'txt', split_axis=0, concat_axis=0)]
  transfers between devices with their start and end apart: 4 -> 4, of which waited for: 4 -> 4; matrix products, arithmetic and copies ran while one was open for 1% -> 2% of each run, Pallas kernels for 0% -> 0%
where the time goes in v1:
time: 427 us; the launch traced here: 426 us
  waiting for transfers between devices  204 us (48%)
  blocking collectives  170 us (40%)
  matrix products  21.4 us (5%)
  between operations  14.4 us (3%)
  other arithmetic  9.6 us (2%)
  starting transfers between devices  4.58 us (1%)
    all_gather x1, waiting for transfers between devices, on_device(): text_full = lax.all_gather(text_pooled, 'img', axis=1, tiled=True)  84.2 us
    all_gather x1, waiting for transfers between devices, on_device(): weight_full = lax.all_gather(text_proj, 'img', axis=0, tiled=True)  76.5 us
    psum x1, blocking collectives, on_device(): lax.psum(jnp.sum(jnp.exp(logits - col_top), axis=0, keepdims=True), 'img')  72.9 us
    pmax x1, blocking collectives, on_device(): col_top = lax.pmax(col_top, 'img')  72.6 us
    all_to_all x1, waiting for transfers between devices, on_device(): parts = lax.all_to_all(parts, 'txt', split_axis=0, concat_axis=0)  32.5 us
    pmax x1, blocking collectives, on_device(): row_top = lax.pmax(row_top, 'txt')  12.4 us
    psum x1, blocking collectives, on_device(): lax.psum(jnp.sum(jnp.exp(logits - row_top), axis=1, keepdims=True), 'txt')  12.4 us
    dot_general x1, matrix products, on_device(): jnp.dot(text_full, weight_full, preferred_element_type=jnp.float32)  10.4 us
  transfers between devices with their start and end apart: 4, of which 4 were waited for; matrix products, arithmetic and copies ran while one was open for 2% of the time, Pallas kernels for 0%

profile of v1, /device:TPU:2, one launch (start us, length us, event | category | flops | bytes accessed | tf_op | source)
XLA Modules:
  0.0 426.2 jit_solution(10597450835491962)
XLA Ops:
  7.2 0.0 all-gather.4.cloned.1.call-start
  7.2 0.7 all-gather.4.cloned.1.call-update
  7.9 0.0 all-gather.8.cloned.1.call-start
  7.9 0.7 all-gather.8.cloned.1.call-update
  8.6 0.0 all-gather.6.cloned.1.call-start
  8.7 0.7 all-gather.6.cloned.1.call-update
  9.4 2.3 stack.2
  11.6 4.5 %all-to-all-start = ((bf16[8,512,208]{1,2,0:T(8,128)(2,1)}), bf16[8,512,208]{1,2,0:T(8,128)(2,1)S(1)}, u32[]{:S(2)}, u32[]{:S(2)}) async-start(bf16[8,512,208]{1,2,0:T(8,128)(2,1)} %stack.2), calls=%async_computation | async-start | bytes 3407872 | tf_op jit(solution)/shard_map/all_to_all | solution.py:20
  16.8 32.5 %all-to-all-done = bf16[8,512,208]{1,2,0:T(8,128)(2,1)S(1)} async-done(((bf16[8,512,208]{1,2,0:T(8,128)(2,1)}), bf16[8,512,208]{1,2,0:T(8,128)(2,1)S(1)}, u32[]{:S(2)}, u32[]{:S(2)}) %all-to-all-start) | async-done | bytes 1703968 | tf_op jit(solution)/shard_map/all_to_all | solution.py:20
  49.3 8.3 %all-gather.4.cloned.1.call-done = bf16[1664,1280]{1,0:T(8,128)(2,1)} async-done(((bf16[208,1280]{1,0:T(8,128)(2,1)}), bf16[1664,1280]{1,0:T(8,128)(2,1)}) %all-gather.4.cloned.1.call-update) | async-done | bytes 4259856 | tf_op jit(solution)/shard_map/all_gather | solution.py:22
  57.6 6.3 %multiply_reduce_fusion.1 = (f32[512]{0:T(512)S(1)}, f32[512,1280]{1,0:T(8,128)}) fusion(bf16[512,1664]{0,1:T(8,128)(2,1)S(1)} %bitcast.17, bf16[1664,1280]{1,0:T(8,128)(2,1)} %all-gather.4.cloned.1.call-done), kind=kOutput, calls=%fused_computation.9 | convolution fusion | flops 2182348288 | bytes 8587264 | tf_op jit(solution)/shard_map/dot_general | solution.py:14
  63.9 0.0 copy-start
  63.9 76.5 %all-gather.8.cloned.1.call-done = bf16[1280,1280]{1,0:T(8,128)(2,1)} async-done(((bf16[40,1280]{1,0:T(8,128)(2,1)}), bf16[1280,1280]{1,0:T(8,128)(2,1)}) %all-gather.8.cloned.1.call-update) | async-done | bytes 3276816 | tf_op jit(solution)/shard_map/all_gather | solution.py:24
  140.4 84.2 %all-gather.6.cloned.1.call-done = bf16[2048,1280]{0,1:T(8,128)(2,1)} async-done(((bf16[2048,40]{0,1:T(8,128)(2,1)}), bf16[2048,1280]{0,1:T(8,128)(2,1)}) %all-gather.6.cloned.1.call-update) | async-done | bytes 5242896 | tf_op jit(solution)/shard_map/all_gather | solution.py:25
  224.6 10.4 %multiply_reduce_fusion = (f32[2048]{0:T(1024)S(1)}, f32[2048,1280]{0,1:T(8,128)S(1)}) fusion(bf16[2048,1280]{0,1:T(8,128)(2,1)} %all-gather.6.cloned.1.call-done, bf16[1280,1280]{1,0:T(8,128)(2,1)} %all-gather.8.cloned.1.call-done), kind=kOutput, calls=%fused_computation.1 | convolution fusion | flops 6716127232 | bytes 19013632 | tf_op jit(solution)/shard_map/dot_general | solution.py:26
  235.0 0.0 copy-done
  235.0 4.7 %fusion.7 = (f32[2048]{0:T(1024)S(1)}, f32[512]{0:T(512)S(1)}, f32[512,2048]{1,0:T(8,128)}) fusion(f32[2048,1280]{0,1:T(8,128)S(1)} %get-tuple-element.9, f32[2048]{0:T(1024)S(1)} %add_rsqrt_fusion, f32[512,1280]{1,0:T(8,128)S(1)} %copy-done, f32[512]{0:T(512)S(1)} %add_rsqrt_fusion.1, f32[]{:T(128)} %bitcast.16), kind=kOutput, calls=%fused_computation.19 | convolution fusion | flops 2697328128 | bytes 17321988 | tf_op jit(solution)/shard_map/dot_general | solution.py:27
  239.7 72.6 %pmax.15 = f32[1,2048]{1,0:T(1,128)S(1)} all-reduce(f32[1,2048]{1,0:T(1,128)S(1)} %bitcast.24), channel_id=1, replica_groups=mesh['img'=32,'txt'=8] {'img'}, use_global_device_ids=true, to_apply=%region_7.0 | all-reduce | flops 2048 | bytes 16384 | tf_op jit(solution)/shard_map/pmax | solution.py:34
  312.3 12.4 %pmax.14 = f32[512,1]{0,1:T(1,128)S(1)} all-reduce(f32[512,1]{0,1:T(1,128)S(1)} %bitcast.25), channel_id=1, replica_groups=mesh['img'=32,'txt'=8] {'txt'}, use_global_device_ids=true, to_apply=%region_3.0 | all-reduce | flops 512 | bytes 4096 | tf_op jit(solution)/shard_map/pmax | solution.py:33
  324.7 3.4 exponential_reduce_fusion
  328.1 12.4 %psum.14 = f32[512,1]{0,1:T(1,128)S(1)} all-reduce(f32[512,1]{0,1:T(1,128)S(1)} %bitcast.22), channel_id=1, replica_groups=mesh['img'=32,'txt'=8] {'txt'}, use_global_device_ids=true, to_apply=%region_5.0 | all-reduce | flops 512 | bytes 4096 | tf_op jit(solution)/shard_map/psum | solution.py:35
  340.6 72.9 %psum.15 = f32[1,2048]{1,0:T(1,128)S(1)} all-reduce(f32[1,2048]{1,0:T(1,128)S(1)} %bitcast.20), channel_id=1, replica_groups=mesh['img'=32,'txt'=8] {'img'}, use_global_device_ids=true, to_apply=%region_9.0 | all-reduce | flops 2048 | bytes 16384 | tf_op jit(solution)/shard_map/psum | solution.py:36
  413.6 6.1 %broadcast_subtract_fusion = (f32[512,2048]{1,0:T(8,128)}, f32[512,2048]{1,0:T(8,128)}) fusion(f32[512,2048]{1,0:T(8,128)} %get-tuple-element.12, f32[2048]{0:T(1024)S(1)} %bitcast.19, f32[512]{0:T(512)S(1)} %bitcast.23), kind=kLoop, calls=%fused_computation.10 | loop fusion | flops 2097152 | bytes 12593152 | tf_op jit(solution)/shard_map/sub | solution.py:38
  (4 shorter events, 0.0 us)
Async XLA Ops:
  7.2 50.4 %all-gather.4.cloned.1.call-start = ((), (), s32[]{:S(2)}) async-start(), calls=%async_computation.1 | async-start | bytes 4792320 | tf_op jit(solution)/shard_map/all_gather | solution.py:22
  7.9 132.5 %all-gather.8.cloned.1.call-start = ((), (), s32[]{:S(2)}) async-start(), calls=%async_computation.3 | async-start | bytes 3379200 | tf_op jit(solution)/shard_map/all_gather | solution.py:24
  8.6 215.9 %all-gather.6.cloned.1.call-start = ((), (), s32[]{:S(2)}) async-start(), calls=%async_computation.2 | async-start | bytes 5406720 | tf_op jit(solution)/shard_map/all_gather | solution.py:25
  11.6 37.6 %all-to-all-start = ((bf16[8,512,208]{1,2,0:T(8,128)(2,1)}), bf16[8,512,208]{1,2,0:T(8,128)(2,1)S(1)}, u32[]{:S(2)}, u32[]{:S(2)}) async-start(bf16[8,512,208]{1,2,0:T(8,128)(2,1)} %stack.2), calls=%async_computation | async-start | bytes 3407872 | tf_op jit(solution)/shard_map/all_to_all | solution.py:20
  63.9 171.1 %copy-start = (f32[512,1280]{1,0:T(8,128)S(1)}, f32[512,1280]{1,0:T(8,128)}, u32[]{:S(2)}) copy-start(f32[512,1280]{1,0:T(8,128)} %get-tuple-element.11) | copy-start | bytes 7864324
Sparse Core Ops, SparseCore 0:
  9.8 47.7 all-gather.3
  60.2 80.1 all-gather.7
  143.0 81.5 all-gather.5
